TPU v7x, 512 devices: a whole 4x4x16 slice. The times are simulated.
512 devices in a mesh: row: 16 (over z), col: 8 (over x, core), rep: 4 (over y).
Axes of the slice: x: 4, y: 4, z: 16, core: 2. Of those that a mesh axis runs over, the one named last changes fastest.
Arguments:
- density: bfloat16 [6144, 6144], P('row', 'col'), as said below
- keep_square: int32 [48, 48], P('row', 'col'), may hold values 0 or 1
- keep_cube: int32 [48, 48], P('row', 'col'), may hold values 0 or 1
Outputs:
- purified: float32 [6144, 6144], P(('row', 'rep'), 'col')
Inputs may be any that keep to these rules, and one draw needn't show every extreme that they name: density is symmetric; its 128 x 128 diagonal blocks are always occupied, any other block may be zero or occupied at any distance from the diagonal.
All inputs are finite; a program needn't handle non-finite values. No bound on the sum of `keep_square` or of `keep_cube` on one device may be relied on, other than what follows from the above.
Results may differ from a plain program's by a relative error of at most 0.002.
Values may be sent and summed in bfloat16 or wider, within the bound.
No kernel may reach another device: no remote copies, remote signals or barrier semaphores. Data moves between devices by JAX's collectives and lax.ppermute only.
A program may use at most 64 MiB of HBM per device.

v0:
```python
import jax
import jax.numpy as jnp
from jax import lax
from jax.sharding import PartitionSpec as P

BLK = 128
TOP = 16384.0
TINY = 1.1754943508222875e-38
PAD = 16


def encode(piece):
    values = piece.astype(jnp.float32)
    largest = jnp.max(jnp.abs(values), axis=0, keepdims=True)
    exponent = jnp.floor(jnp.log2(jnp.maximum(largest, TINY)))
    coded = (values * jnp.exp2(-exponent) * TOP).astype(jnp.float16)
    header = jnp.broadcast_to(exponent, (PAD, piece.shape[1])).astype(jnp.float16)
    return jnp.concatenate([coded, header], axis=0)


def decode(coded, count):
    parts = coded.reshape(count, -1, coded.shape[1]).astype(jnp.float32)
    height = parts.shape[1] - PAD
    scale = jnp.exp2(parts[:, height : height + 1, :])
    values = (parts[:, :height, :] * (1.0 / TOP) * scale).astype(jnp.bfloat16)
    return values.reshape(count * height, coded.shape[1])


def local(density, keep_square, keep_cube):
    tile_rows, tile_cols = density.shape
    reps = lax.axis_size("rep")
    row_count = lax.axis_size("row")
    col_count = lax.axis_size("col")
    rep = lax.axis_index("rep")
    own = tile_rows // reps
    halves = tile_cols // tile_rows

    def section(array):
        cut = [
            lax.dynamic_slice_in_dim(array, half * tile_rows + rep * own, own, 0)
            for half in range(halves)
        ]
        return jnp.concatenate(cut, axis=0)

    right_piece = lax.dynamic_slice_in_dim(density, rep * own, own, 0)
    left_piece = section(density.T)
    left = decode(lax.all_gather(encode(left_piece), "col", axis=0, tiled=True), col_count)
    right = decode(lax.all_gather(encode(right_piece), "row", axis=0, tiled=True), row_count)

    def contract(a, b):
        return lax.dot_general(a, b, (((0,), (0,)), ((), ())), preferred_element_type=jnp.float32)

    partial = contract(right, left)
    partial = partial.reshape(halves, reps, own, tile_rows).transpose(1, 0, 2, 3)
    partial = partial.reshape(reps, halves * own, tile_rows)
    square_t = jnp.sum(lax.all_to_all(partial, "rep", 0, 0), axis=0)
    mask_rows = section(jnp.repeat(keep_square.T.astype(jnp.float32), BLK, axis=0))
    square_t = square_t * jnp.repeat(mask_rows, BLK, axis=1)
    low = decode(
        lax.all_gather(encode(square_t.astype(jnp.bfloat16)), "col", axis=0, tiled=True), col_count
    )
    cube = contract(low, right)
    mask = jnp.repeat(jnp.repeat(keep_cube.astype(jnp.float32), BLK, axis=0), BLK, axis=1)
    placed = jnp.zeros((tile_cols, tile_rows), jnp.float32)
    for half in range(halves):
        placed = lax.dynamic_update_slice_in_dim(
            placed, square_t[half * own : (half + 1) * own], half * tile_rows + rep * own, 0
        )
    total = 3.0 * placed.T - 2.0 * cube * mask
    pieces = lax.all_to_all(total.reshape(reps, own, tile_cols), "rep", 0, 0)
    return jnp.sum(pieces, axis=0)


def solution(mesh):
    return jax.shard_map(
        local,
        mesh=mesh,
        in_specs=(P("row", "col"), P("row", "col"), P("row", "col")),
        out_specs=P(("row", "rep"), "col"),
        check_vma=False,
    )
```

profile of v0, /device:TPU:1, one launch (start us, length us, event | category | flops | bytes accessed | tf_op | source)
XLA Modules:
  0.0 156.7 jit_solution(12126970050853005048)
XLA Ops:
  0.0 0.9 fusion.11
  1.0 1.0 fusion.13
  2.0 49.8 %all-gather.3 = f16[1792,768]{1,0:T(8,128)(2,1)S(1)} all-gather(f16[112,768]{1,0:T(8,128)(2,1)S(1)} %pad_maximum_fusion.3), channel_id=1, replica_groups=mesh['row'=16,'col'=8,'rep'=4] {'row'}, dimensions={0}, use_global_device_ids=true | all-gather | bytes 2924544 | tf_op jit(solution)/shard_map/all_gather | solution.py:48
  51.8 0.5 convert.3
  52.4 0.1 fusion.15
  52.5 0.5 fusion
  53.0 2.4 %copy.12 = bf16[1536,768]{0,1:T(8,128)(2,1)} copy(bf16[1536,768]{1,0:T(8,128)(2,1)S(1)} %bitcast.59) | data formatting | bytes 4718592 | tf_op jit(solution)/shard_map/reshape | solution.py:26
  55.5 1.1 dynamic-slice_bitcast_fusion.1
  56.6 0.2 fusion.5
  56.9 0.2 fusion.7
  57.1 0.1 broadcast_in_dim.35
  57.2 0.1 pad_maximum_fusion.1
  57.3 0.2 copy.13
  57.5 21.3 %all-gather.4 = f16[1664,384]{1,0:T(8,128)(2,1)S(1)} all-gather(f16[208,384]{1,0:T(8,128)(2,1)S(1)} %copy.13), channel_id=1, replica_groups=mesh['row'=16,'col'=8,'rep'=4] {'col'}, dimensions={0}, use_global_device_ids=true | all-gather | bytes 1437696 | tf_op jit(solution)/shard_map/all_gather | solution.py:47
  78.9 0.2 convert.4
  79.1 0.0 copy-start
  79.1 0.2 fusion.2
  79.3 1.4 copy-done
  80.7 1.4 convolution_bitcast_fusion
  82.1 1.1 copy.14
  83.3 4.4 %all-to-all-start = ((f32[4,192,384]{2,1,0:T(8,128)}), f32[4,192,384]{2,1,0:T(8,128)}, u32[]{:S(2)}, u32[]{:S(2)}) async-start(f32[4,192,384]{2,1,0:T(8,128)} %bitcast.13), calls=%async_computation | async-start | bytes 2359296 | tf_op jit(solution)/shard_map/all_to_all | solution.py:56
  87.7 0.0 copy-done.1
  87.7 0.1 broadcast_bitcast_fusion.1
  87.8 0.0 copy-done.2
  87.8 0.1 copy.17
  87.9 0.1 broadcast_bitcast_fusion
  87.9 1.1 broadcast_in_dim.40
  89.0 1.6 %copy.18 = f32[384,768]{1,0:T(8,128)S(1)} copy(f32[384,768]{0,1:T(8,128)} %bitcast.66) | data formatting | bytes 2359296 | tf_op jit(solution)/shard_map/reshape | solution.py:63
  90.7 0.1 constant_dynamic-slice_fusion.1
  90.8 0.1 pad_maximum_fusion.4
  90.8 13.1 %all-to-all-done = f32[4,192,384]{2,1,0:T(8,128)} async-done(((f32[4,192,384]{2,1,0:T(8,128)}), f32[4,192,384]{2,1,0:T(8,128)}, u32[]{:S(2)}, u32[]{:S(2)}) %all-to-all-start) | async-done | bytes 1179680 | tf_op jit(solution)/shard_map/all_to_all | solution.py:56
  103.9 2.1 %reduce_sum.18 = f32[192,384]{1,0:T(8,128)} reduce(f32[4,192,384]{2,1,0:T(8,128)} %all-to-all-done, f32[]{:T(128)} %constant.15.clone.1), dimensions={0}, to_apply=%region_2.0 | reduce | flops 221184 | bytes 1474564 | tf_op jit(solution)/shard_map/reduce_sum | solution.py:56
  106.0 1.9 %copy.15 = f32[192,384]{0,1:T(8,128)} copy(f32[192,384]{1,0:T(8,128)} %reduce_sum.18) | data formatting | bytes 589824 | tf_op jit(solution)/shard_map/reduce_sum | solution.py:56
  107.9 1.1 fusion.8
  109.0 0.8 fusion.23
  109.8 0.1 fusion.10
  110.0 0.1 broadcast_in_dim.38
  110.1 0.8 pad_maximum_fusion.2
  110.9 1.7 %copy.16 = f16[208,384]{1,0:T(8,128)(2,1)} copy(f16[208,384]{0,1:T(8,128)(2,1)} %pad_maximum_fusion.2) | data formatting | bytes 319488 | tf_op jit(solution)/shard_map/concatenate | solution.py:18
  112.6 15.4 %all-gather.5 = f16[1664,384]{1,0:T(8,128)(2,1)S(1)} all-gather(f16[208,384]{1,0:T(8,128)(2,1)} %copy.16), channel_id=1, replica_groups=mesh['row'=16,'col'=8,'rep'=4] {'col'}, dimensions={0}, use_global_device_ids=true | all-gather | bytes 1437696 | tf_op jit(solution)/shard_map/all_gather | solution.py:60
  128.0 0.2 convert.5
  128.2 1.2 fusion.1
  129.4 1.1 broadcast_in_dim.16
  130.6 2.0 %dynamic_update_slice.6 = f32[768,384]{0,1:T(8,128)} dynamic-update-slice(f32[768,384]{0,1:T(8,128)} %broadcast_in_dim.16, f32[96,384]{0,1:T(8,128)} %get-tuple-element.10, s32[]{:T(128)S(6)} %select_n.14, s32[]{:T(128)} %constant.18.clone.1) | dynamic-update-slice | bytes 294916 | tf_op jit(solution)/shard_map/dynamic_update_slice | solution.py:66
  132.5 1.9 %dynamic_update_slice.7 = f32[768,384]{0,1:T(8,128)} dynamic-update-slice(f32[768,384]{0,1:T(8,128)} %dynamic_update_slice.6, f32[96,384]{0,1:T(8,128)} %get-tuple-element.9, s32[]{:T(128)S(6)} %select_n.15, s32[]{:T(128)} %constant.18.clone.1) | dynamic-update-slice | bytes 294916 | tf_op jit(solution)/shard_map/dynamic_update_slice | solution.py:66
  134.5 2.8 %fusion.4 = f32[384,768]{1,0:T(8,128)S(1)} fusion(f32[384,768]{1,0:T(8,128)S(1)} %copy.18, bf16[1536,384]{1,0:T(8,128)(2,1)} %bitcast.65, bf16[1536,768]{1,0:T(8,128)(2,1)S(1)} %bitcast.60, f32[768,384]{0,1:T(8,128)} %dynamic_update_slice.7), kind=kOutput, calls=%fused_computation.9 | convolution fusion | flops 907149312 | bytes 7077888 | tf_op jit(solution)/shard_map/dot_general | solution.py:51
  137.3 18.7 %all_to_all.10 = f32[4,96,768]{2,1,0:T(8,128)S(1)} all-to-all(f32[4,96,768]{2,1,0:T(8,128)S(1)} %bitcast.64), channel_id=1, replica_groups=mesh['row'=16,'col'=8,'rep'=4] {'rep'}, dimensions={0} | all-to-all | bytes 2359296 | tf_op jit(solution)/shard_map/all_to_all | solution.py:70
  155.9 0.8 reduce_sum.19
  (16 shorter events, 0.2 us)
Async XLA Ops:
  79.1 1.7 %copy-start = (bf16[1536,768]{0,1:T(8,128)(2,1)S(1)}, bf16[1536,768]{0,1:T(8,128)(2,1)}, u32[]{:S(2)}) copy-start(bf16[1536,768]{0,1:T(8,128)(2,1)} %copy.12) | copy-start | bytes 7077892
  83.2 4.4 %copy-start.1 = (s32[3,6]{1,0:T(4,128)S(1)}, s32[3,6]{1,0:T(4,128)}, u32[]{:S(2)}) copy-start(s32[3,6]{1,0:T(4,128)} %param.4) | copy-start | bytes 220
  83.2 4.5 %copy-start.2 = (s32[3,6]{1,0:T(4,128)S(1)}, s32[3,6]{1,0:T(4,128)}, u32[]{:S(2)}) copy-start(s32[3,6]{1,0:T(4,128)} %param.5) | copy-start | bytes 220
  83.3 20.7 %all-to-all-start = ((f32[4,192,384]{2,1,0:T(8,128)}), f32[4,192,384]{2,1,0:T(8,128)}, u32[]{:S(2)}, u32[]{:S(2)}) async-start(f32[4,192,384]{2,1,0:T(8,128)} %bitcast.13), calls=%async_computation | async-start | bytes 2359296 | tf_op jit(solution)/shard_map/all_to_all | solution.py:56
where the time goes:
time: 157 us
  blocking collectives  105 us (67%)
  local copies, waits for them, and re-layouts  19.1 us (12%)
  waiting for transfers between devices  13.1 us (8%)
  other arithmetic  10.5 us (7%)
  starting transfers between devices  4.39 us (3%)
  matrix products  4.17 us (3%)
    all_gather x1, blocking collectives, local(): lax.all_gather(encode(right_piece), 'row', axis=0, tiled=True)  49.8 us
    all_gather x1, blocking collectives, local(): lax.all_gather(encode(left_piece), 'col', axis=0, tiled=True)  21.3 us
    all_to_all x1, blocking collectives, local(): pieces = lax.all_to_all(total.reshape(reps, own, tile_cols), 'rep', 0, 0)  18.7 us
    all_gather x1, blocking collectives, local(): lax.all_gather(encode(square_t.astype(jnp.bfloat16)), 'col', axis=0, tile...  15.4 us
    all_to_all x1, waiting for transfers between devices, local(): square_t = jnp.sum(lax.all_to_all(partial, 'rep', 0, 0), axis=0)  13.1 us
    all_to_all x1, starting transfers between devices, local(): square_t = jnp.sum(lax.all_to_all(partial, 'rep', 0, 0), axis=0)  4.39 us
    dot_general x2, matrix products, contract(): lax.dot_general(a, b, (((0,), (0,)), ((), ())), preferred_element_type=jn...  4.17 us
    dynamic_update_slice x2, local copies, waits for them, and re-layouts, local(): lax.dynamic_update_slice_in_dim(placed, square_t[half * own:(half + 1) *...  3.9 us
  transfers between devices with their start and end apart: 1, of which 1 were waited for; matrix products, arithmetic and copies ran while one was open for 2% of the time, Pallas kernels for 0%

commit v1 on v0

--- a/solution.py
+++ b/solution.py
@@ -45,7 +45,13 @@
     right_piece = lax.dynamic_slice_in_dim(density, rep * own, own, 0)
     left_piece = section(density.T)
     left = decode(lax.all_gather(encode(left_piece), "col", axis=0, tiled=True), col_count)
-    right = decode(lax.all_gather(encode(right_piece), "row", axis=0, tiled=True), row_count)
+    right = decode(
+        jnp.concatenate(
+            lax.all_to_all(jnp.stack([encode(right_piece)] * lax.axis_size("row")), "row", 0, 0),
+            axis=0,
+        ),
+        row_count,
+    )
 
     def contract(a, b):
         return lax.dot_general(a, b, (((0,), (0,)), ((), ())), preferred_element_type=jnp.float32)

time: 157 us -> 223 us (1.42)
  waiting for transfers between devices: 13.1 us -> 110 us
  blocking collectives: 105 us -> 53.9 us
  starting transfers between devices: 4.39 us -> 20 us
    all_to_all x0 -> x1, waiting for transfers between devices: none -> 101 us  [local(): lax.all_to_all(jnp.stack([encode(right_piece)] * lax.axis_size('row')), '...]
    all_gather x1 -> x0, blocking collectives: 49.8 us -> none  [local(): lax.all_gather(encode(right_piece), 'row', axis=0, tiled=True)]
    all_to_all x0 -> x1, starting transfers between devices: none -> 15.7 us  [local(): lax.all_to_all(jnp.stack([encode(right_piece)] * lax.axis_size('row')), '...]
    all_gather x1, blocking collectives: 21.3 us -> 15 us  [local(): lax.all_gather(encode(left_piece), 'col', axis=0, tiled=True)]
    all_gather x1, blocking collectives: 15.4 us -> 20.2 us  [local(): lax.all_gather(encode(square_t.astype(jnp.bfloat16)), 'col', axis=0, tile...]
    all_to_all x1, waiting for transfers between devices: 13.1 us -> 8.84 us  [local(): square_t = jnp.sum(lax.all_to_all(partial, 'rep', 0, 0), axis=0)]
    dot_general x0 -> x1, local copies, waits for them, and re-layouts: none -> 2.44 us  [contract(): lax.dot_general(a, b, (((0,), (0,)), ((), ())), preferred_element_type=jn...]
    reshape x1 -> x0, local copies, waits for them, and re-layouts: 2.44 us -> none  [decode(): return values.reshape(count * height, coded.shape[1])]
  transfers between devices with their start and end apart: 1 -> 2, of which waited for: 1 -> 2; matrix products, arithmetic and copies ran while one was open for 2% -> 3% of each run, Pallas kernels for 0% -> 0%
where the time goes in v1:
time: 223 us; the launch traced here: 222 us
  waiting for transfers between devices  110 us (49%)
  blocking collectives  53.9 us (24%)
  local copies, waits for them, and re-layouts  20.2 us (9%)
  starting transfers between devices  20 us (9%)
  other arithmetic  11.9 us (5%)
  matrix products  5.84 us (3%)
    all_to_all x1, waiting for transfers between devices, local(): lax.all_to_all(jnp.stack([encode(right_piece)] * lax.axis_size('row')), '...  101 us
    all_gather x1, blocking collectives, local(): lax.all_gather(encode(square_t.astype(jnp.bfloat16)), 'col', axis=0, tile...  20.2 us
    all_to_all x1, blocking collectives, local(): pieces = lax.all_to_all(total.reshape(reps, own, tile_cols), 'rep', 0, 0)  18.6 us
    all_to_all x1, starting transfers between devices, local(): lax.all_to_all(jnp.stack([encode(right_piece)] * lax.axis_size('row')), '...  15.7 us
    all_gather x1, blocking collectives, local(): lax.all_gather(encode(left_piece), 'col', axis=0, tiled=True)  15 us
    all_to_all x1, waiting for transfers between devices, local(): square_t = jnp.sum(lax.all_to_all(partial, 'rep', 0, 0), axis=0)  8.84 us
    dot_general x2, matrix products, contract(): lax.dot_general(a, b, (((0,), (0,)), ((), ())), preferred_element_type=jn...  5.84 us
  transfers between devices with their start and end apart: 2, of which 2 were waited for; matrix products, arithmetic and copies ran while one was open for 3% of the time, Pallas kernels for 0%

profile of v1, /device:TPU:1, one launch (start us, length us, event | category | flops | bytes accessed | tf_op | source)
XLA Modules:
  0.0 222.2 jit_solution(4039199704161431435)
XLA Ops:
  0.0 0.9 fusion.11
  1.0 1.0 fusion.13
  2.0 1.7 stack.2
  3.7 15.7 %all-to-all-start = ((f16[16,112,768]{2,1,0:T(8,128)(2,1)}), f16[16,112,768]{2,1,0:T(8,128)(2,1)S(1)}, u32[]{:S(2)}, u32[]{:S(2)}) async-start(f16[16,112,768]{2,1,0:T(8,128)(2,1)} %stack.2), calls=%async_computation | async-start | bytes 5505024 | tf_op jit(solution)/shard_map/all_to_all | solution.py:50
  19.5 1.2 dynamic-slice_bitcast_fusion.1
  20.6 0.2 fusion.5
  20.9 0.2 fusion.7
  21.1 0.1 broadcast_in_dim.35
  21.2 0.1 pad_maximum_fusion.1
  21.3 0.2 copy.23
  21.5 15.0 %all-gather.2 = f16[1664,384]{1,0:T(8,128)(2,1)S(1)} all-gather(f16[208,384]{1,0:T(8,128)(2,1)S(1)} %copy.23), channel_id=1, replica_groups=mesh['row'=16,'col'=8,'rep'=4] {'col'}, dimensions={0}, use_global_device_ids=true | all-gather | bytes 1437696 | tf_op jit(solution)/shard_map/all_gather | solution.py:47
  36.6 0.2 convert.2
  36.8 1.3 fusion.2
  38.1 101.4 %all-to-all-done = f16[16,112,768]{2,1,0:T(8,128)(2,1)S(1)} async-done(((f16[16,112,768]{2,1,0:T(8,128)(2,1)}), f16[16,112,768]{2,1,0:T(8,128)(2,1)S(1)}, u32[]{:S(2)}, u32[]{:S(2)}) %all-to-all-start) | async-done | bytes 2752544 | tf_op jit(solution)/shard_map/all_to_all | solution.py:50
  139.4 0.9 copy_convert_fusion
  140.4 0.6 fusion
  141.0 0.7 copy.21
  141.7 2.4 %copy.22 = bf16[768,1536]{1,0:T(8,128)(2,1)} copy(bf16[768,1536]{0,1:T(8,128)(2,1)S(1)} %bitcast.56) | data formatting | bytes 4718592 | tf_op jit(solution)/shard_map/dot_general | solution.py:57
  144.2 3.0 %convolution_bitcast_fusion = f32[4,2,96,384]{3,2,0,1:T(8,128)S(1)} fusion(bf16[2,4,96,1536]{3,2,1,0:T(8,128)(2,1)} %bitcast.63, bf16[1536,384,1,1]{1,0,3,2:T(8,128)(2,1)S(1)} %bitcast.64), kind=kOutput, calls=%fused_computation.9 | convolution fusion | flops 905969664 | bytes 4718592 | tf_op jit(solution)/shard_map/dot_general | solution.py:57
  147.2 0.0 copy-start.1
  147.2 0.0 copy-start.2
  147.3 1.1 copy.24
  148.4 4.3 %all-to-all-start.1 = ((f32[4,192,384]{2,1,0:T(8,128)}), f32[4,192,384]{2,1,0:T(8,128)}, u32[]{:S(2)}, u32[]{:S(2)}) async-start(f32[4,192,384]{2,1,0:T(8,128)} %bitcast.12), calls=%async_computation.1 | async-start | bytes 2359296 | tf_op jit(solution)/shard_map/all_to_all | solution.py:62
  152.7 0.1 broadcast_bitcast_fusion.1
  152.8 0.1 copy.27
  152.9 0.1 broadcast_bitcast_fusion
  152.9 1.1 broadcast_in_dim.40
  154.0 1.6 copy.28
  155.7 0.1 constant_dynamic-slice_fusion.1
  155.8 0.1 pad_maximum_fusion.4
  155.8 8.8 %all-to-all-done.1 = f32[4,192,384]{2,1,0:T(8,128)} async-done(((f32[4,192,384]{2,1,0:T(8,128)}), f32[4,192,384]{2,1,0:T(8,128)}, u32[]{:S(2)}, u32[]{:S(2)}) %all-to-all-start.1) | async-done | bytes 1179680 | tf_op jit(solution)/shard_map/all_to_all | solution.py:62
  164.7 2.1 reduce_sum.18
  166.8 1.9 copy.25
  168.6 1.1 fusion.8
  169.8 0.8 fusion.24
  170.6 0.1 fusion.10
  170.7 0.1 broadcast_in_dim.38
  170.8 0.8 pad_maximum_fusion.2
  171.6 1.7 copy.26
  173.4 20.2 %all-gather.3 = f16[1664,384]{1,0:T(8,128)(2,1)S(1)} all-gather(f16[208,384]{1,0:T(8,128)(2,1)} %copy.26), channel_id=1, replica_groups=mesh['row'=16,'col'=8,'rep'=4] {'col'}, dimensions={0}, use_global_device_ids=true | all-gather | bytes 1437696 | tf_op jit(solution)/shard_map/all_gather | solution.py:66
  193.5 0.2 convert.3
  193.8 1.2 fusion.1
  195.0 1.1 broadcast_in_dim.16
  196.1 2.0 dynamic_update_slice.6
  198.1 1.9 dynamic_update_slice.7
  200.0 2.8 %fusion.4 = f32[384,768]{1,0:T(8,128)S(1)} fusion(f32[384,768]{1,0:T(8,128)S(1)} %copy.28, bf16[1536,384]{1,0:T(8,128)(2,1)} %bitcast.61, bf16[1536,768]{1,0:T(8,128)(2,1)S(1)} %bitcast.57, f32[768,384]{0,1:T(8,128)} %dynamic_update_slice.7), kind=kOutput, calls=%fused_computation.10 | convolution fusion | flops 907149312 | bytes 7077888 | tf_op jit(solution)/shard_map/dot_general | solution.py:57
  202.8 18.6 %all_to_all.15 = f32[4,96,768]{2,1,0:T(8,128)S(1)} all-to-all(f32[4,96,768]{2,1,0:T(8,128)S(1)} %bitcast.60), channel_id=1, replica_groups=mesh['row'=16,'col'=8,'rep'=4] {'rep'}, dimensions={0} | all-to-all | bytes 2359296 | tf_op jit(solution)/shard_map/all_to_all | solution.py:76
  221.5 0.8 reduce_sum.19
  (18 shorter events, 0.2 us)
Async XLA Ops:
  3.7 135.7 %all-to-all-start = ((f16[16,112,768]{2,1,0:T(8,128)(2,1)}), f16[16,112,768]{2,1,0:T(8,128)(2,1)S(1)}, u32[]{:S(2)}, u32[]{:S(2)}) async-start(f16[16,112,768]{2,1,0:T(8,128)(2,1)} %stack.2), calls=%async_computation | async-start | bytes 5505024 | tf_op jit(solution)/shard_map/all_to_all | solution.py:50
  141.7 2.5 %copy-start = (bf16[8,192,384]{2,1,0:T(8,128)(2,1)S(1)}, bf16[8,192,384]{2,1,0:T(8,128)(2,1)}, u32[]{:S(2)}) copy-start(bf16[8,192,384]{2,1,0:T(8,128)(2,1)} %fusion.2) | copy-start | bytes 3538948
  147.2 5.4 %copy-start.1 = (s32[3,6]{1,0:T(4,128)S(1)}, s32[3,6]{1,0:T(4,128)}, u32[]{:S(2)}) copy-start(s32[3,6]{1,0:T(4,128)} %param.4) | copy-start | bytes 220
  147.2 5.5 %copy-start.2 = (s32[3,6]{1,0:T(4,128)S(1)}, s32[3,6]{1,0:T(4,128)}, u32[]{:S(2)}) copy-start(s32[3,6]{1,0:T(4,128)} %param.5) | copy-start | bytes 220
  148.4 16.3 %all-to-all-start.1 = ((f32[4,192,384]{2,1,0:T(8,128)}), f32[4,192,384]{2,1,0:T(8,128)}, u32[]{:S(2)}, u32[]{:S(2)}) async-start(f32[4,192,384]{2,1,0:T(8,128)} %bitcast.12), calls=%async_computation.1 | async-start | bytes 2359296 | tf_op jit(solution)/shard_map/all_to_all | solution.py:62
